TPU v7x, 512 devices: a whole 4x4x16 slice. The times are simulated.
512 devices in a mesh: seq: 32 (over y, z_hi, core), chan: 16 (over x, z_lo).
Axes of the slice: x: 4, y: 4, z: 16 (z_hi: 4, z_lo: 4; z = z_hi * 4 + z_lo), core: 2. Of those that a mesh axis runs over, the one named last changes fastest.
Arguments:
- outer_gate: bfloat16 [16384, 2048], P('seq', 'chan'), may hold values from -6 to 6
- inner_gate: bfloat16 [16384, 2048], P('seq', 'chan'), may hold values from -6 to 6
- values: bfloat16 [16384, 2048], P('seq', 'chan'), may hold values from -6 to 6
- filters: bfloat16 [16384, 16], P('seq'), may hold values from -0.046875 to 0.046875
- cotangent: bfloat16 [16384, 2048], P('seq', 'chan'), may hold values from -6 to 6
Outputs:
- layer_out: bfloat16 [16384, 2048], P('seq', 'chan')
- outer_grad: bfloat16 [16384, 2048], P('seq', 'chan')
- inner_grad: bfloat16 [16384, 2048], P('seq', 'chan')
- value_grad: bfloat16 [16384, 2048], P('seq', 'chan')
- filter_grad: float32 [16384, 16], P('seq')
All inputs are finite; a program needn't handle non-finite values.
Results may differ from a plain program's by a relative error of at most 0.0051.
Values may be sent and summed in bfloat16 or wider, within the bound.
A program may use at most 128 MiB of HBM per device.

v0:
```python
import math

import jax
import jax.numpy as jnp
from jax import lax
from jax.sharding import PartitionSpec as P

HIGHEST = lax.Precision.HIGHEST


def tables(rows_out, rows_in, period, direction):
    row_index = lax.broadcasted_iota(jnp.int32, (rows_out, rows_in), 0)
    col_index = lax.broadcasted_iota(jnp.int32, (rows_out, rows_in), 1)
    phase_arg = (
        direction * 2.0 * math.pi / period * (row_index * col_index % period).astype(jnp.float32)
    )
    return (jnp.cos(phase_arg), jnp.sin(phase_arg))


def column_forward(signal):
    blocks = signal.shape[0]
    cosine, sine_tab = tables(2 * blocks, blocks, 2 * blocks, -1)
    pattern = "kr,rsw->ksw"
    return (
        jnp.einsum(pattern, cosine, signal, precision=HIGHEST),
        jnp.einsum(pattern, sine_tab, signal, precision=HIGHEST),
    )


def rotate(real_part, imag_part, freq_rows, time_cols, period, direction):
    phase_arg = (
        direction
        * 2.0
        * math.pi
        / period
        * (freq_rows[:, None] * time_cols[None, :] % period).astype(jnp.float32)
    )
    cosine = jnp.cos(phase_arg)
    sine_tab = jnp.sin(phase_arg)
    cosine = cosine[:, :, None]
    sine_tab = sine_tab[:, :, None]
    return (real_part * cosine - imag_part * sine_tab, real_part * sine_tab + imag_part * cosine)


def row_transform(real_part, imag_part, direction):
    extent = real_part.shape[1]
    cosine, sine_tab = tables(extent, extent, extent, direction)
    pattern = "kn,rnw->rkw"

    def multiply(matrix, operand):
        return jnp.einsum(pattern, matrix, operand, precision=HIGHEST)

    return (
        multiply(cosine, real_part) - multiply(sine_tab, imag_part),
        multiply(sine_tab, real_part) + multiply(cosine, imag_part),
    )


def column_inverse(real_part, imag_part, period):
    rows_all = real_part.shape[0]
    cosine, sine_tab = tables(rows_all // 2, rows_all, rows_all, 1)
    pattern = "nk,ksw->nsw"

    def multiply(matrix, operand):
        return jnp.einsum(pattern, matrix, operand, precision=HIGHEST)

    factor = 1.0 / period
    real_out = (multiply(cosine, real_part) - multiply(sine_tab, imag_part)) * factor
    imag_out = (multiply(sine_tab, real_part) + multiply(cosine, imag_part)) * factor
    return (real_out, imag_out)


def combine_spectra(inner_re, inner_im, upper_re, upper_im, filt_re, filt_im):
    forward_re = filt_re * inner_re - filt_im * inner_im
    forward_im = filt_re * inner_im + filt_im * inner_re
    backward_re = filt_re * upper_re + filt_im * upper_im
    backward_im = filt_re * upper_im - filt_im * upper_re
    cross_re = inner_re * upper_re + inner_im * upper_im
    cross_im = inner_re * upper_im - inner_im * upper_re
    return (forward_re, forward_im, backward_re, backward_im, cross_re, cross_im)


def on_device(outer_gate, inner_gate, values, filters, cotangent):
    tok_rows = outer_gate.shape[0]
    chan_cols = outer_gate.shape[1]
    filt_count = filters.shape[1]
    seq_count = lax.axis_size("seq")
    seq_rank = lax.axis_index("seq")
    period = 2 * seq_count * tok_rows
    inner = (inner_gate.astype(jnp.float32) * values.astype(jnp.float32)).astype(jnp.bfloat16)
    upstream = (cotangent.astype(jnp.float32) * outer_gate.astype(jnp.float32)).astype(jnp.bfloat16)
    piece_len = tok_rows // seq_count
    signals = jnp.concatenate([inner, upstream, filters], axis=1)
    breadth = signals.shape[1]
    columns = lax.all_to_all(
        signals.reshape(seq_count, piece_len, breadth),
        "seq",
        split_axis=0,
        concat_axis=0,
        tiled=True,
    )
    real_part, imag_part = column_forward(columns.astype(jnp.float32))
    freq_rows = jnp.arange(2 * seq_count, dtype=jnp.int32)
    time_cols = seq_rank * piece_len + jnp.arange(piece_len, dtype=jnp.int32)
    real_part, imag_part = rotate(real_part, imag_part, freq_rows, time_cols, period, -1)
    rows_re, rows_im = (
        lax.all_to_all(real_part, "seq", split_axis=0, concat_axis=1, tiled=True),
        lax.all_to_all(imag_part, "seq", split_axis=0, concat_axis=1, tiled=True),
    )
    spec_re, spec_im = row_transform(rows_re, rows_im, -1)
    copies = chan_cols // filt_count
    filt_re = jnp.tile(spec_re[:, :, 2 * chan_cols :], (1, 1, copies))
    filt_im = jnp.tile(spec_im[:, :, 2 * chan_cols :], (1, 1, copies))
    fwd_re, fwd_im, bwd_re, bwd_im, cross_re, cross_im = combine_spectra(
        spec_re[:, :, :chan_cols],
        spec_im[:, :, :chan_cols],
        spec_re[:, :, chan_cols : 2 * chan_cols],
        spec_im[:, :, chan_cols : 2 * chan_cols],
        filt_re,
        filt_im,
    )
    local_rows = spec_re.shape[0]
    cross_re = cross_re.reshape(local_rows, tok_rows, copies, filt_count).sum(axis=2)
    cross_im = cross_im.reshape(local_rows, tok_rows, copies, filt_count).sum(axis=2)
    cross_re, cross_im = lax.psum((cross_re, cross_im), "chan")
    back_re = jnp.concatenate([fwd_re, bwd_re, cross_re], axis=2)
    back_im = jnp.concatenate([fwd_im, bwd_im, cross_im], axis=2)
    back_re, back_im = row_transform(back_re, back_im, 1)
    freq_rows = local_rows * seq_rank + jnp.arange(local_rows, dtype=jnp.int32)
    time_cols = jnp.arange(tok_rows, dtype=jnp.int32)
    back_re, back_im = rotate(back_re, back_im, freq_rows, time_cols, period, 1)
    cols_re, cols_im = (
        lax.all_to_all(back_re, "seq", split_axis=1, concat_axis=0, tiled=True),
        lax.all_to_all(back_im, "seq", split_axis=1, concat_axis=0, tiled=True),
    )
    time_re, time_im = column_inverse(cols_re, cols_im, period)
    time_re = lax.all_to_all(time_re, "seq", split_axis=0, concat_axis=1, tiled=True)
    convolved = time_re[0, :, :chan_cols]
    backward = time_re[0, :, chan_cols : 2 * chan_cols]
    correlated = time_re[0, :, 2 * chan_cols :]
    layer_out = (outer_gate.astype(jnp.float32) * convolved).astype(jnp.bfloat16)
    outer_grad = (cotangent.astype(jnp.float32) * convolved).astype(jnp.bfloat16)
    inner_grad = (backward * values.astype(jnp.float32)).astype(jnp.bfloat16)
    value_grad = (backward * inner_gate.astype(jnp.float32)).astype(jnp.bfloat16)
    grad_scale = float(tok_rows * seq_count * chan_cols * lax.axis_size("chan") // filt_count) ** (
        -0.5
    )
    filter_grad = correlated * grad_scale
    return (layer_out, outer_grad, inner_grad, value_grad, filter_grad)


def solution(mesh):
    placed = (
        P("seq", "chan"),
        P("seq", "chan"),
        P("seq", "chan"),
        P("seq", None),
        P("seq", "chan"),
    )
    return jax.shard_map(
        on_device,
        mesh=mesh,
        in_specs=placed,
        out_specs=(
            P("seq", "chan"),
            P("seq", "chan"),
            P("seq", "chan"),
            P("seq", "chan"),
            P("seq", None),
        ),
        check_vma=False,
    )
```

profile of v0, /device:TPU:1, one launch (start us, length us, event | category | flops | bytes accessed | tf_op | source)
XLA Modules:
  0.0 672.4 jit_solution(15731640095895072511)
XLA Ops:
  7.2 0.8 copy.36
  8.0 1.2 fusion.46
  9.2 0.8 pad_maximum_fusion.6
  10.0 19.4 %all-to-all-start = ((bf16[32,16,272]{2,1,0:T(8,128)(2,1)}), bf16[32,16,272]{2,1,0:T(8,128)(2,1)S(1)}, u32[]{:S(2)}, u32[]{:S(2)}) async-start(bf16[32,16,272]{2,1,0:T(8,128)(2,1)} %bitcast.2), calls=%async_computation | async-start | bytes 786432 | tf_op jit(solution)/shard_map/all_to_all | solution.py:95
  29.4 0.1 fusion.86
  29.5 23.3 %all-to-all-done = bf16[32,16,272]{2,1,0:T(8,128)(2,1)S(1)} async-done(((bf16[32,16,272]{2,1,0:T(8,128)(2,1)}), bf16[32,16,272]{2,1,0:T(8,128)(2,1)S(1)}, u32[]{:S(2)}, u32[]{:S(2)}) %all-to-all-start) | async-done | bytes 278560 | tf_op jit(solution)/shard_map/all_to_all | solution.py:95
  52.8 0.9 fusion.42
  53.7 1.3 multiply_add_fusion
  55.1 2.0 copy.39
  57.1 8.0 %all-to-all-start.1 = ((f32[64,16,272]{2,1,0:T(8,128)}), f32[64,16,272]{2,1,0:T(8,128)S(1)}, u32[]{:S(2)}, u32[]{:S(2)}) async-start(f32[64,16,272]{2,1,0:T(8,128)} %copy.39), calls=%async_computation.1 | async-start | bytes 3145728 | tf_op jit(solution)/shard_map/all_to_all | solution.py:107
  65.1 2.1 copy.42
  67.2 35.1 %all-to-all-done.1 = f32[64,16,272]{2,1,0:T(8,128)S(1)} async-done(((f32[64,16,272]{2,1,0:T(8,128)}), f32[64,16,272]{2,1,0:T(8,128)S(1)}, u32[]{:S(2)}, u32[]{:S(2)}) %all-to-all-start.1) | async-done | bytes 1114144 | tf_op jit(solution)/shard_map/all_to_all | solution.py:107
  102.2 45.8 %all-to-all-start.2 = ((f32[64,16,272]{2,1,0:T(8,128)}), f32[64,16,272]{2,1,0:T(8,128)S(1)}, u32[]{:S(2)}, u32[]{:S(2)}) async-start(f32[64,16,272]{2,1,0:T(8,128)} %copy.42), calls=%async_computation.2 | async-start | bytes 3145728 | tf_op jit(solution)/shard_map/all_to_all | solution.py:108
  148.1 0.2 all-reduce.3.cloned.1.call-start
  148.3 0.1 copy.40
  148.4 8.9 %fusion.11 = f32[2,272,512]{2,1,0:T(8,128)S(1)} fusion(f32[2,512,272]{2,1,0:T(8,128)S(1)} %bitcast.122), kind=kOutput, calls=%fused_computation.33 | convolution fusion | flops 1714946048 | bytes 2228224 | tf_op jit(solution)/shard_map/kn,rnw->rkw/dot_general | solution.py:51
  157.4 9.4 %fusion.15 = f32[2,272,512]{2,1,0:T(8,128)} fusion(f32[2,512,272]{2,1,0:T(8,128)S(1)} %bitcast.123), kind=kOutput, calls=%fused_computation.37 | convolution fusion | flops 1714946048 | bytes 2228224 | tf_op jit(solution)/shard_map/kn,rnw->rkw/dot_general | solution.py:51
  166.8 49.0 %all-to-all-done.2 = f32[64,16,272]{2,1,0:T(8,128)S(1)} async-done(((f32[64,16,272]{2,1,0:T(8,128)}), f32[64,16,272]{2,1,0:T(8,128)S(1)}, u32[]{:S(2)}, u32[]{:S(2)}) %all-to-all-start.2) | async-done | bytes 1114144 | tf_op jit(solution)/shard_map/all_to_all | solution.py:108
  215.8 0.1 copy.43
  215.9 1.1 copy-done.7
  217.1 9.2 %fusion.1 = f32[2,512,272]{1,2,0:T(8,128)S(1)} fusion(f32[2,272,512]{2,1,0:T(8,128)S(1)} %copy-done.7, f32[2,512,272]{2,1,0:T(8,128)S(1)} %bitcast.120), kind=kOutput, calls=%fused_computation.10 | convolution fusion | flops 1715224576 | bytes 3342336 | tf_op jit(solution)/shard_map/kn,rnw->rkw/dot_general | solution.py:51
  226.2 9.4 %fusion = f32[2,512,272]{1,2,0:T(8,128)S(1)} fusion(f32[2,272,512]{2,1,0:T(8,128)S(1)} %fusion.11, f32[2,512,272]{2,1,0:T(8,128)S(1)} %bitcast.121), kind=kOutput, calls=%fused_computation.8 | convolution fusion | flops 1715224576 | bytes 3342336 | tf_op jit(solution)/shard_map/kn,rnw->rkw/dot_general | solution.py:51
  235.6 0.4 fusion.22
  236.1 0.7 reduce_sum.18
  236.8 0.7 reduce_sum.19
  237.5 0.2 fusion.88
  237.7 161.0 %all-reduce.3.cloned.1.call-done = (f32[2,512,16]{1,2,0:T(8,128)}, f32[2,512,16]{1,2,0:T(8,128)}) async-done(((f32[2,512,16]{1,2,0:T(8,128)}, f32[2,512,16]{1,2,0:T(8,128)}), (f32[2,512,16]{1,2,0:T(8,128)}, f32[2,512,16]{1,2,0:T(8,128)})) %all-reduce.3.cloned.1.call-update) | async-done | bytes 131088 | tf_op jit(solution)/shard_map/psum | solution.py:125
  398.6 6.7 fusion.5
  405.4 6.0 fusion.9
  411.4 5.8 convolution_add_fusion
  417.1 7.3 %add_bitcast_fusion = (f32[2,512,272]{1,2,0:T(8,128)S(1)}, f32[2,512,272]{1,2,0:T(8,128)S(1)}) fusion(f32[2,272,512]{2,1,0:T(8,128)S(1)} %convolution_add_fusion, f32[2,512]{1,0:T(2,128)S(1)} %get-tuple-element.37, f32[2,512]{1,0:T(2,128)S(1)} %get-tuple-element.36, f32[2,272,512]{2,1,0:T(8,128)S(1)} %fusion.9, f32[2,512,16]{1,2,0:T(8,128)S(1)} %copy-done.5, ...), kind=kOutput, calls=%fused_computation.23 | convolution fusion | flops 1717452800 | bytes 5578752 | tf_op jit(solution)/shard_map/kn,rnw->rkw/dot_general | solution.py:51
  424.4 2.2 copy.50
  426.7 25.2 %all-to-all-start.4 = ((f32[2,512,272]{2,0,1:T(2,128)}), f32[2,512,272]{2,0,1:T(2,128)S(1)}, u32[]{:S(2)}, u32[]{:S(2)}) async-start(f32[2,512,272]{2,0,1:T(2,128)} %copy.50), calls=%async_computation.4 | async-start | bytes 3145728 | tf_op jit(solution)/shard_map/all_to_all | solution.py:134
  451.9 2.2 copy.47
  454.1 72.9 %all-to-all-done.4 = f32[2,512,272]{2,0,1:T(2,128)S(1)} async-done(((f32[2,512,272]{2,0,1:T(2,128)}), f32[2,512,272]{2,0,1:T(2,128)S(1)}, u32[]{:S(2)}, u32[]{:S(2)}) %all-to-all-start.4) | async-done | bytes 1114144 | tf_op jit(solution)/shard_map/all_to_all | solution.py:134
  527.1 7.9 %all-to-all-start.3 = ((f32[2,512,272]{2,0,1:T(2,128)}), f32[2,512,272]{2,0,1:T(2,128)S(1)}, u32[]{:S(2)}, u32[]{:S(2)}) async-start(f32[2,512,272]{2,0,1:T(2,128)} %copy.47), calls=%async_computation.3 | async-start | bytes 3145728 | tf_op jit(solution)/shard_map/all_to_all | solution.py:133
  534.9 0.1 copy.51
  535.0 2.3 copy.52
  537.4 2.4 all_to_all.80
  539.8 68.7 %all-to-all-done.3 = f32[2,512,272]{2,0,1:T(2,128)S(1)} async-done(((f32[2,512,272]{2,0,1:T(2,128)}), f32[2,512,272]{2,0,1:T(2,128)S(1)}, u32[]{:S(2)}, u32[]{:S(2)}) %all-to-all-start.3) | async-done | bytes 1114144 | tf_op jit(solution)/shard_map/all_to_all | solution.py:133
  608.6 1.2 copy.49
  609.8 2.2 all_to_all.76
  612.1 2.3 fusion.60
  614.4 0.9 fusion.2
  615.4 0.5 copy.53
  615.9 47.8 %all_to_all.89 = f32[32,16,272]{2,1,0:T(8,128)S(1)} all-to-all(f32[32,16,272]{2,1,0:T(8,128)S(1)} %copy.53), channel_id=1, replica_groups=mesh['seq'=32,'chan'=16] {'seq'}, dimensions={0} | all-to-all | bytes 1114112 | tf_op jit(solution)/shard_map/all_to_all | solution.py:137
  663.8 0.8 fusion.45
  664.6 0.7 copy.54
  (22 shorter events, 0.2 us)
Async XLA Ops:
  10.0 42.8 %all-to-all-start = ((bf16[32,16,272]{2,1,0:T(8,128)(2,1)}), bf16[32,16,272]{2,1,0:T(8,128)(2,1)S(1)}, u32[]{:S(2)}, u32[]{:S(2)}) async-start(bf16[32,16,272]{2,1,0:T(8,128)(2,1)} %bitcast.2), calls=%async_computation | async-start | bytes 786432 | tf_op jit(solution)/shard_map/all_to_all | solution.py:95
  57.1 45.1 %all-to-all-start.1 = ((f32[64,16,272]{2,1,0:T(8,128)}), f32[64,16,272]{2,1,0:T(8,128)S(1)}, u32[]{:S(2)}, u32[]{:S(2)}) async-start(f32[64,16,272]{2,1,0:T(8,128)} %copy.39), calls=%async_computation.1 | async-start | bytes 3145728 | tf_op jit(solution)/shard_map/all_to_all | solution.py:107
  102.2 113.6 %all-to-all-start.2 = ((f32[64,16,272]{2,1,0:T(8,128)}), f32[64,16,272]{2,1,0:T(8,128)S(1)}, u32[]{:S(2)}, u32[]{:S(2)}) async-start(f32[64,16,272]{2,1,0:T(8,128)} %copy.42), calls=%async_computation.2 | async-start | bytes 3145728 | tf_op jit(solution)/shard_map/all_to_all | solution.py:108
  148.1 250.6 %all-reduce.3.cloned.1.call-start = ((), (), s32[]{:S(2)}) async-start(), calls=%async_computation.6 | async-start | bytes 262144 | tf_op jit(solution)/shard_map/psum | solution.py:125
  215.8 1.2 copy-start.7
  236.1 175.3 %copy-start.4 = (f32[2,512,128]{1,2,0:T(8,128)}, f32[2,512,128]{1,2,0:T(8,128)S(1)}, u32[]{:S(2)}) copy-start(f32[2,512,128]{1,2,0:T(8,128)S(1)} %get-tuple-element.25) | copy-start | bytes 1572868
  398.6 6.7 copy-start.6
  405.4 6.0 copy-start.5
  426.7 100.4 %all-to-all-start.4 = ((f32[2,512,272]{2,0,1:T(2,128)}), f32[2,512,272]{2,0,1:T(2,128)S(1)}, u32[]{:S(2)}, u32[]{:S(2)}) async-start(f32[2,512,272]{2,0,1:T(2,128)} %copy.50), calls=%async_computation.4 | async-start | bytes 3145728 | tf_op jit(solution)/shard_map/all_to_all | solution.py:134
  527.1 81.4 %all-to-all-start.3 = ((f32[2,512,272]{2,0,1:T(2,128)}), f32[2,512,272]{2,0,1:T(2,128)S(1)}, u32[]{:S(2)}, u32[]{:S(2)}) async-start(f32[2,512,272]{2,0,1:T(2,128)} %copy.47), calls=%async_computation.3 | async-start | bytes 3145728 | tf_op jit(solution)/shard_map/all_to_all | solution.py:133
  615.8 47.9 %copy-start = (bf16[512,128]{1,0:T(8,128)(2,1)S(1)}, bf16[512,128]{1,0:T(8,128)(2,1)}, u32[]{:S(2)}) copy-start(bf16[512,128]{1,0:T(8,128)(2,1)} %param.6) | copy-start | bytes 393220
  615.8 47.9 %copy-start.1 = (bf16[512,128]{1,0:T(8,128)(2,1)S(1)}, bf16[512,128]{1,0:T(8,128)(2,1)}, u32[]{:S(2)}) copy-start(bf16[512,128]{1,0:T(8,128)(2,1)} %param.7) | copy-start | bytes 393220
  615.8 47.9 %copy-start.2 = (bf16[512,128]{1,0:T(8,128)(2,1)S(1)}, bf16[512,128]{1,0:T(8,128)(2,1)}, u32[]{:S(2)}) copy-start(bf16[512,128]{1,0:T(8,128)(2,1)} %param.5) | copy-start | bytes 393220
  615.9 47.9 %copy-start.3 = (bf16[512,128]{1,0:T(8,128)(2,1)S(1)}, bf16[512,128]{1,0:T(8,128)(2,1)}, u32[]{:S(2)}) copy-start(bf16[512,128]{1,0:T(8,128)(2,1)} %param.9) | copy-start | bytes 393220
Sparse Core Ops, SparseCore 0:
  237.6 160.9 all-reduce.2
where the time goes:
time: 678 us; the launch traced here: 672 us
  waiting for transfers between devices  410 us (60%)
  starting transfers between devices  106 us (16%)
  matrix products  68.1 us (10%)
  blocking collectives  47.8 us (7%)
  local copies, waits for them, and re-layouts  20.4 us (3%)
  between operations  14.6 us (2%)
    psum x1, waiting for transfers between devices, on_device(): cross_re, cross_im = lax.psum((cross_re, cross_im), 'chan')  161 us
    all_to_all x1, waiting for transfers between devices, on_device(): lax.all_to_all(back_im, 'seq', split_axis=1, concat_axis=0, tiled=True)  72.9 us
    all_to_all x1, waiting for transfers between devices, on_device(): lax.all_to_all(back_re, 'seq', split_axis=1, concat_axis=0, tiled=True)  68.7 us
    dot_general x10, matrix products, multiply(): return jnp.einsum(pattern, matrix, operand, precision=HIGHEST)  65.9 us
    all_to_all x1, waiting for transfers between devices, on_device(): lax.all_to_all(imag_part, 'seq', split_axis=0, concat_axis=1, tiled=True)  49 us
    all_to_all x1, blocking collectives, on_device(): lax.all_to_all(time_re, 'seq', split_axis=0, concat_axis=1, tiled=True)  47.8 us
    all_to_all x1, starting transfers between devices, on_device(): lax.all_to_all(imag_part, 'seq', split_axis=0, concat_axis=1, tiled=True)  45.8 us
    all_to_all x1, waiting for transfers between devices, on_device(): lax.all_to_all(real_part, 'seq', split_axis=0, concat_axis=1, tiled=True)  35.1 us
  transfers between devices with their start and end apart: 6, of which 6 were waited for; matrix products, arithmetic and copies ran while one was open for 4% of the time, Pallas kernels for 0%

commit v1 on v0

v1 whole, which is shorter than its diff:
```python
import jax
import jax.numpy as jnp
from jax import lax
from jax.experimental import pallas as pl
from jax.experimental.pallas import tpu as pltpu
from jax.sharding import PartitionSpec as P

BF16 = jnp.bfloat16
F32 = jnp.float32
MESH = pl.DeviceIdType.MESH
SEQ = 32
CHAN = 16
TAPS = 16
LANES = 128
ROWS = 256


def nn(a, b):
    return lax.dot_general(a, b, (((1,), (0,)), ((), ())), preferred_element_type=F32)


def nt(a, b):
    return lax.dot_general(a, b, (((1,), (1,)), ((), ())), preferred_element_type=F32)


def iota(shape, axis):
    return lax.broadcasted_iota(jnp.int32, shape, axis)


def one_hot(hit):
    return jnp.where(hit, 1.0, 0.0).astype(BF16)


def eye(n):
    return one_hot(iota((n, n), 0) == iota((n, n), 1))


def flip(n):
    return one_hot(iota((n, n), 0) + iota((n, n), 1) == n - 1)


def routing():
    row, col = iota((512, 512), 0), iota((512, 512), 1)
    s, p, b, k = row >> 4, (row >> 3) & 1, (row >> 2) & 1, row & 3
    wanted = (2 * b + 1 - p) * LANES + (s >> 1) + TAPS * (4 * (s & 1) + k)
    return one_hot(col == wanted)


def stack_tokens(x, order):
    return jnp.concatenate([x[LANES * n : LANES * (n + 1)] for n in order], axis=1)


def shear(x):
    return pltpu.roll(x, 0, 1, stride=1, stride_axis=0)


def upper():
    return iota((LANES, LANES), 1) >= iota((LANES, LANES), 0)


def toeplitz(taps, w):
    w[0:LANES, :] = jnp.zeros((LANES, LANES), BF16)
    keep = upper()

    def body(s, before):
        for n in range(4):
            h = taps[s, n : n + 1, :].astype(F32)
            now = shear(jnp.broadcast_to(h, (LANES, LANES)))
            at = pl.multiple_of((4 * s + n + 1) * LANES, LANES)
            w[pl.ds(at, LANES), :] = jnp.where(keep, now, before).astype(BF16)
            before = now
        return before

    lax.fori_loop(0, SEQ, body, jnp.zeros((LANES, LANES), F32))


def unpack(slots):
    wide = slots[...].astype(F32)
    return jnp.concatenate(
        [wide[:, 0:8].reshape(ROWS, LANES), wide[:, 8:16].reshape(ROWS, LANES)], axis=1
    )


def pack(y):
    return jnp.concatenate(
        [y[:, :LANES].reshape(SEQ, 8, LANES), y[:, LANES:].reshape(SEQ, 8, LANES)], axis=1
    ).astype(BF16)


def spread_x(x, xs):
    xs[0:ROWS, :] = jnp.zeros((ROWS, 1024), BF16)
    row = iota((ROWS, ROWS), 0)
    for d in range(4):
        moved = x if d == 0 else jnp.where(row >= 4 * d, pltpu.roll(x, 4 * d, 0), 0.0)
        xs[ROWS:, ROWS * d : ROWS * (d + 1)] = moved.astype(BF16)


def spread_u(u, us):
    us[ROWS:, :] = jnp.zeros((us.shape[0] - ROWS, 1024), BF16)
    row = iota((ROWS, ROWS), 0)
    for d in range(4):
        moved = u if d == 0 else jnp.where(row < ROWS - 4 * d, pltpu.roll(u, ROWS - 4 * d, 0), 0.0)
        us[0:ROWS, ROWS * d : ROWS * (d + 1)] = moved.astype(BF16)


def lag_weights(w, group):
    at = pl.multiple_of(group * 1024, 1024)
    return jnp.concatenate(
        [w[pl.ds(at, 1024), :], w[pl.ds(pl.multiple_of(at + LANES, LANES), 1024), :]], axis=1
    )


def convolve(xs, w, y):
    y[...] = jnp.zeros((ROWS, ROWS), F32)
    for quarter in range(4):
        size = ROWS - 64 * quarter

        def body(g, _):
            at = pl.multiple_of(ROWS - 16 * g, 16)
            y[64 * quarter :, :] += nn(xs[pl.ds(at, size), :], lag_weights(w, 4 * quarter + g))
            return 0

        lax.fori_loop(0, 4, body, 0)


def convolve_back(us, w, y):
    y[...] = jnp.zeros((ROWS, ROWS), F32)
    for quarter in range(4):
        size = ROWS - 64 * quarter

        def body(g, _):
            group = 4 * quarter + g
            at = pl.multiple_of(16 * group, 16)
            y[0:size, :] += nn(us[pl.ds(at, size), :], lag_weights(w, group))
            return 0

        lax.fori_loop(0, 4, body, 0)


def correlate(ut, xs, out):
    keep = upper()

    def emit(before, now, group, e):
        line = jnp.sum(jnp.where(keep, before, now), axis=0, keepdims=True)
        out[2 * group + (e + 6) // 4, (e + 6) % 4, :] = line[0]

    def body(group, carry):
        before, edge = carry
        at = pl.multiple_of(ROWS - 16 * group, 16)
        pairs = nn(ut[...], xs[pl.ds(at, ROWS), :])
        for e in range(8):
            low = pairs[0:LANES, LANES * e : LANES * (e + 1)]
            high = edge if e == 0 else pairs[LANES:, LANES * (e - 1) : LANES * e]
            now = shear(low + high)
            emit(before, now, group, e)
            before = now
        return before, pairs[LANES:, LANES * 7 :]

    zero = jnp.zeros((LANES, LANES), F32)
    before, edge = lax.fori_loop(0, 16, body, (zero, zero))
    now = shear(edge)
    emit(before, now, 16, 0)
    emit(now, zero, 16, 1)


def product(a, b):
    return a[...].astype(F32) * b[...].astype(F32)


def kernel(
    og, ig, va, taps, ct,
    layer_out, outer_grad, inner_grad, value_grad, filter_grad,
    send_h, send_x, send_u, send_c, send_b, send_g, send_t,
    recv_h, recv_x, recv_u, recv_c, recv_b, recv_g, recv_t,
    w, xs, us, ut, y, route, sems_out, sems_in,
):
    s, c = lax.axis_index("seq"), lax.axis_index("chan")
    f, half = s // 2, s % 2
    own_part = 16 * half + c
    is_self = s == own_part

    def device(seq, chan):
        return {"seq": seq, "chan": chan}

    barrier = pltpu.get_barrier_semaphore()

    def greet(seq, chan):
        pl.semaphore_signal(barrier, inc=1, device_id=device(seq, chan), device_id_type=MESH)

    def greet_seq(i, _):
        greet(lax.rem(s + i, SEQ), c)
        return 0

    def greet_chan(i, _):
        greet(s, lax.rem(c + i, CHAN))
        greet(2 * f + 1 - half, lax.rem(c + i, CHAN))
        return 0

    def greet_source(i, _):
        @pl.when(jnp.logical_not(jnp.logical_and(is_self, i == f)))
        def _():
            greet(2 * i + s // 16, lax.rem(s, 16))

        return 0

    lax.fori_loop(1, SEQ, greet_seq, 0)
    lax.fori_loop(1, CHAN, greet_chan, 0)
    greet(2 * f + 1 - half, c)
    lax.fori_loop(0, TAPS, greet_source, 0)

    taps_flat = stack_tokens(taps[...], range(4))
    row, col = iota((64, 64), 0), iota((64, 64), 1)
    taps_rows = nt(one_hot(col == (row & 3) * TAPS + (row >> 2)), taps_flat).astype(BF16)
    for i in range(TAPS):
        send_h[i] = taps_rows[4 * i : 4 * (i + 1)]
    route[...] = routing()
    inner = stack_tokens(product(ig, va).astype(BF16), range(4))
    send_x[...] = nt(route[...], inner).astype(BF16).reshape(SEQ, 16, LANES)
    upstream = stack_tokens(product(ct, og).astype(BF16), (1, 0, 3, 2))
    upstream = nn(flip(LANES), upstream).astype(BF16)
    send_u[...] = nt(route[...], upstream).astype(BF16).reshape(SEQ, 16, LANES)

    @pl.when(is_self)
    def _():
        pl.semaphore_wait(barrier, 2 * (SEQ - 1) + TAPS - 1)

    @pl.when(jnp.logical_not(is_self))
    def _():
        pl.semaphore_wait(barrier, 2 * (SEQ - 1) + TAPS)

    def copy(src, dst, n, seq, chan):
        return pltpu.make_async_remote_copy(
            src_ref=src, dst_ref=dst, send_sem=sems_out.at[n], recv_sem=sems_in.at[n],
            device_id=device(seq, chan), device_id_type=MESH,
        )

    def exchange(src, dst, n, slot):
        def body(i, _):
            to = lax.rem(s + i, SEQ)
            copy(src.at[slot(to)], dst.at[s], n, to, c).start()
            return 0

        lax.fori_loop(1, SEQ, body, 0)
        dst[s] = src[slot(s)]

    def whole(ref, count, n):
        part = ref.at[pl.ds(0, count)]
        return copy(part, part, n, s, c)

    exchange(send_h, recv_h, 0, lambda to: to // 2)
    exchange(send_x, recv_x, 1, lambda to: to)
    exchange(send_u, recv_u, 2, lambda to: to)

    whole(recv_h, SEQ - 1, 0).wait_recv()
    toeplitz(recv_h, w)
    whole(recv_x, SEQ - 1, 1).wait_recv()
    spread_x(unpack(recv_x), xs)
    convolve(xs, w, y)
    send_c[...] = pack(y[...])
    exchange(send_c, recv_c, 3, lambda to: to)

    whole(recv_u, SEQ - 1, 2).wait_recv()
    u = unpack(recv_u)
    spread_u(u, us)
    ut[...] = nt(eye(ROWS), u.astype(BF16)).astype(BF16)
    convolve_back(us, w, y)
    send_b[...] = pack(y[...])
    exchange(send_b, recv_b, 4, lambda to: to)

    correlate(ut, xs, send_g)

    def parts_out(i, _):
        to = lax.rem(c + i, CHAN)
        here = c * 2 + half

        @pl.when(i > 0)
        def _():
            copy(send_g.at[2 + 16 * half + to], recv_g.at[here], 5, s, to).start()

        other = 1 - half
        copy(send_g.at[2 + 16 * other + to], recv_g.at[here], 5, 2 * f + other, to).start()
        return 0

    lax.fori_loop(0, CHAN, parts_out, 0)
    recv_g[c * 2 + half] = send_g[2 + own_part]

    whole(recv_c, SEQ - 1, 3).wait_recv()
    tokens = nt(eye(LANES), recv_c[...].reshape(512, LANES)).astype(BF16)
    result = nn(tokens, route[...])
    for n in range(4):
        here = pl.ds(LANES * (n ^ 1), LANES)
        part = result[:, LANES * n : LANES * (n + 1)]
        layer_out[here, :] = (og[here, :].astype(F32) * part).astype(BF16)
        outer_grad[here, :] = (ct[here, :].astype(F32) * part).astype(BF16)

    whole(recv_g, SEQ - 1, 5).wait_recv()
    send_t[0] = jnp.sum(recv_g[...], axis=0)

    def total_out(i, _):
        to = lax.rem(c + i, CHAN)

        @pl.when(jnp.logical_not(jnp.logical_and(is_self, i == 0)))
        def _():
            copy(send_t.at[0], recv_t.at[f], 6, own_part, to).start()

        return 0

    lax.fori_loop(0, CHAN, total_out, 0)

    @pl.when(is_self)
    def _():
        recv_t[f] = send_t[0]

    whole(recv_b, SEQ - 1, 4).wait_recv()
    tokens = nt(flip(LANES), recv_b[...].reshape(512, LANES)).astype(BF16)
    result = nn(tokens, route[...])
    for n in range(4):
        here = pl.ds(LANES * n, LANES)
        part = result[:, LANES * n : LANES * (n + 1)]
        inner_grad[here, :] = (part * va[here, :].astype(F32)).astype(BF16)
        value_grad[here, :] = (part * ig[here, :].astype(F32)).astype(BF16)

    @pl.when(is_self)
    def _():
        whole(recv_t, TAPS - 1, 6).wait()

    @pl.when(jnp.logical_not(is_self))
    def _():
        whole(recv_t, TAPS, 6).wait()

    scale = float(512 * SEQ * LANES * CHAN // TAPS) ** -0.5
    back = flip(LANES).astype(F32)
    for n in range(4):
        part = lax.dot_general(
            back, recv_t[:, n, :], (((1,), (1,)), ((), ())),
            precision=lax.Precision.HIGHEST, preferred_element_type=F32,
        )
        filter_grad[LANES * n : LANES * (n + 1), :] = part * scale

    whole(recv_h, SEQ - 1, 0).wait_send()
    for n, ref in ((1, recv_x), (2, recv_u), (3, recv_c), (4, recv_b), (5, recv_g)):
        whole(ref, SEQ - 1, n).wait_send()


def on_device(outer_gate, inner_gate, values, filters, cotangent):
    wide = jax.ShapeDtypeStruct((512, LANES), BF16)
    slots = pltpu.VMEM((SEQ, 16, LANES), BF16)
    vmem = pl.BlockSpec(memory_space=pltpu.VMEM)
    return pl.pallas_call(
        kernel,
        out_shape=(wide, wide, wide, wide, jax.ShapeDtypeStruct((512, TAPS), F32)),
        in_specs=[vmem] * 5,
        out_specs=(vmem,) * 5,
        scratch_shapes=[
            pltpu.VMEM((TAPS, 4, LANES), BF16),
            slots, slots, slots, slots,
            pltpu.VMEM((2 + SEQ, 4, LANES), F32),
            pltpu.VMEM((1, 4, LANES), F32),
            pltpu.VMEM((SEQ, 4, LANES), BF16),
            slots, slots, slots, slots,
            pltpu.VMEM((SEQ, 4, LANES), F32),
            pltpu.VMEM((TAPS, 4, LANES), F32),
            pltpu.VMEM((129 * LANES, LANES), BF16),
            pltpu.VMEM((2 * ROWS, 1024), BF16),
            pltpu.VMEM((ROWS + 64, 1024), BF16),
            pltpu.VMEM((ROWS, ROWS), BF16),
            pltpu.VMEM((ROWS, ROWS), F32),
            pltpu.VMEM((512, 512), BF16),
            pltpu.SemaphoreType.DMA((7,)),
            pltpu.SemaphoreType.DMA((7,)),
        ],
        compiler_params=pltpu.CompilerParams(
            collective_id=0, has_side_effects=True, vmem_limit_bytes=40 * 2**20
        ),
    )(outer_gate, inner_gate, values, filters, cotangent)


def solution(mesh):
    placed = (P("seq", "chan"),) * 3 + (P("seq", None), P("seq", "chan"))
    return jax.shard_map(
        on_device,
        mesh=mesh,
        in_specs=placed,
        out_specs=(P("seq", "chan"),) * 4 + (P("seq", None),),
        check_vma=False,
    )
```

time: 678 us -> 73.4 us (0.11)
  waiting for transfers between devices: 410 us -> 0 us
  starting transfers between devices: 106 us -> 0 us
  matrix products: 68.1 us -> 0 us
  Pallas kernels: 0 us -> 65.6 us
  blocking collectives: 47.8 us -> 0 us
  between operations: 14.6 us -> 0.65 us
  local copies, waits for them, and re-layouts: 20.4 us -> 6.96 us
    all_to_all x5 -> x0, waiting for transfers between devices: 249 us -> none  [the longest x1 72.9 us: on_device(): lax.all_to_all(back_im, 'seq', split_axis=1, concat_axis=0, tiled=True)]
    psum x1 -> x0, waiting for transfers between devices: 161 us -> none  [on_device(): cross_re, cross_im = lax.psum((cross_re, cross_im), 'chan')]
    all_to_all x5 -> x0, starting transfers between devices: 106 us -> none  [the longest x1 45.8 us: on_device(): lax.all_to_all(imag_part, 'seq', split_axis=0, concat_axis=1, tiled=True)]
    dot_general x12 -> x0, matrix products: 68.1 us -> none  [the longest x10 65.9 us: multiply(): return jnp.einsum(pattern, matrix, operand, precision=HIGHEST)]
    pallas_call x0 -> x1, Pallas kernels: none -> 65.6 us  [on_device(): pl.pallas_call(kernel, out_shape=(wide, wide, wide, wide, jax.ShapeDtypeS...]
    all_to_all x1 -> x0, blocking collectives: 47.8 us -> none  [on_device(): lax.all_to_all(time_re, 'seq', split_axis=0, concat_axis=1, tiled=True)]
    all_to_all x8 -> x0, local copies, waits for them, and re-layouts: 8.6 us -> none  [the longest x3 4.81 us: on_device(): lax.all_to_all(back_im, 'seq', split_axis=1, concat_axis=0, tiled=True)]
  transfers between devices with their start and end apart: 6 -> 0, of which waited for: 6 -> 0; matrix products, arithmetic and copies ran while one was open for 4% -> 0% of each run, Pallas kernels for 0% -> 0%
where the time goes in v1:
time: 73.4 us; the launch traced here: 73.2 us
  Pallas kernels  65.6 us (89%)
  local copies, waits for them, and re-layouts  6.96 us (9%)
    pallas_call x1, Pallas kernels, on_device(): pl.pallas_call(kernel, out_shape=(wide, wide, wide, wide, jax.ShapeDtypeS...  65.6 us
    unnamed x13, local copies, waits for them, and re-layouts  6.24 us

profile of v1, /device:TPU:1, one launch (start us, length us, event | category | flops | bytes accessed | tf_op | source)
XLA Modules:
  0.0 73.2 jit_solution(13920594504651785585)
XLA Ops:
  0.6 0.0 copy-start
  0.6 0.9 %copy.10.taps = bf16[512,16]{1,0:T(8,128)(2,1)S(1)} copy(bf16[512,16]{0,1:T(8,128)(2,1)} %param.8) | data formatting | bytes 32768 | tf_op args[3]
  1.5 0.0 copy-done
  1.6 0.0 copy-start.1
  1.6 0.9 %copy-done.1 = bf16[512,128]{1,0:T(8,128)(2,1)S(1)} copy-done((bf16[512,128]{1,0:T(8,128)(2,1)S(1)}, bf16[512,128]{1,0:T(8,128)(2,1)}, u32[]{:S(2)}) %copy-start.1) | copy-done | bytes 131096
  2.5 0.0 copy-start.2
  2.5 0.9 %copy-done.2 = bf16[512,128]{1,0:T(8,128)(2,1)S(1)} copy-done((bf16[512,128]{1,0:T(8,128)(2,1)S(1)}, bf16[512,128]{1,0:T(8,128)(2,1)}, u32[]{:S(2)}) %copy-start.2) | copy-done | bytes 131096
  3.4 0.0 copy-start.3
  3.4 0.9 %copy-done.3 = bf16[512,128]{1,0:T(8,128)(2,1)S(1)} copy-done((bf16[512,128]{1,0:T(8,128)(2,1)S(1)}, bf16[512,128]{1,0:T(8,128)(2,1)}, u32[]{:S(2)}) %copy-start.3) | copy-done | bytes 131096
  4.3 65.6 %shard_map.92 = (bf16[512,128]{1,0:T(8,128)(2,1)S(1)}, bf16[512,128]{1,0:T(8,128)(2,1)S(1)}, bf16[512,128]{1,0:T(8,128)(2,1)S(1)}, bf16[512,128]{1,0:T(8,128)(2,1)S(1)}, f32[512,16]{1,0:T(8,128)S(1)}) custom-call(bf16[512,128]{1,0:T(8,128)(2,1)S(1)} %copy-done, bf16[512,128]{1,0:T(8,128)(2,1)S(1)} %copy-done.1, bf16[512,128]{1,0:T(8,128)(2,1)S(1)} %copy-done.2, ...), custom_call_target="tpu_custom_call" | custom-call | tf_op jit(solution)/shard_map/pallas_call | solution.py:349
  69.9 0.7 copy.11
  70.6 0.7 copy.16
  71.3 0.7 copy.17
  71.9 0.7 copy.18
  72.6 0.7 copy.19
Async XLA Ops:
  0.6 0.9 %copy-start = (bf16[512,128]{1,0:T(8,128)(2,1)S(1)}, bf16[512,128]{1,0:T(8,128)(2,1)}, u32[]{:S(2)}) copy-start(bf16[512,128]{1,0:T(8,128)(2,1)} %og.1) | copy-start | bytes 393220
  1.6 0.9 %copy-start.1 = (bf16[512,128]{1,0:T(8,128)(2,1)S(1)}, bf16[512,128]{1,0:T(8,128)(2,1)}, u32[]{:S(2)}) copy-start(bf16[512,128]{1,0:T(8,128)(2,1)} %ig.1) | copy-start | bytes 393220
  2.5 0.9 %copy-start.2 = (bf16[512,128]{1,0:T(8,128)(2,1)S(1)}, bf16[512,128]{1,0:T(8,128)(2,1)}, u32[]{:S(2)}) copy-start(bf16[512,128]{1,0:T(8,128)(2,1)} %va.1) | copy-start | bytes 393220
  3.4 0.9 %copy-start.3 = (bf16[512,128]{1,0:T(8,128)(2,1)S(1)}, bf16[512,128]{1,0:T(8,128)(2,1)}, u32[]{:S(2)}) copy-start(bf16[512,128]{1,0:T(8,128)(2,1)} %ct.1) | copy-start | bytes 393220

commit v2 on v1

--- a/solution.py
+++ b/solution.py
@@ -1,3 +1,5 @@
+import functools
+
 import jax
 import jax.numpy as jnp
 from jax import lax
@@ -71,7 +73,7 @@
             before = now
         return before
 
-    lax.fori_loop(0, SEQ, body, jnp.zeros((LANES, LANES), F32))
+    lax.fori_loop(0, SEQ, body, jnp.zeros((LANES, LANES), F32), unroll=8)
 
 
 def unpack(slots):
@@ -120,7 +122,7 @@
             y[64 * quarter :, :] += nn(xs[pl.ds(at, size), :], lag_weights(w, 4 * quarter + g))
             return 0
 
-        lax.fori_loop(0, 4, body, 0)
+        lax.fori_loop(0, 4, body, 0, unroll=4)
 
 
 def convolve_back(us, w, y):
@@ -134,7 +136,7 @@
             y[0:size, :] += nn(us[pl.ds(at, size), :], lag_weights(w, group))
             return 0
 
-        lax.fori_loop(0, 4, body, 0)
+        lax.fori_loop(0, 4, body, 0, unroll=4)
 
 
 def correlate(ut, xs, out):
@@ -157,7 +159,7 @@
         return before, pairs[LANES:, LANES * 7 :]
 
     zero = jnp.zeros((LANES, LANES), F32)
-    before, edge = lax.fori_loop(0, 16, body, (zero, zero))
+    before, edge = lax.fori_loop(0, 16, body, (zero, zero), unroll=16)
     now = shear(edge)
     emit(before, now, 16, 0)
     emit(now, zero, 16, 1)
@@ -168,11 +170,11 @@
 
 
 def kernel(
-    og, ig, va, taps, ct,
-    layer_out, outer_grad, inner_grad, value_grad, filter_grad,
+    og_far, ig_far, va_far, taps_far, ct_far,
+    sums, grads,
     send_h, send_x, send_u, send_c, send_b, send_g, send_t,
     recv_h, recv_x, recv_u, recv_c, recv_b, recv_g, recv_t,
-    w, xs, us, ut, y, route, sems_out, sems_in,
+    og, ig, va, taps, ct, w, xs, us, ut, y, route, sems_out, sems_in, fetched,
 ):
     s, c = lax.axis_index("seq"), lax.axis_index("chan")
     f, half = s // 2, s % 2
@@ -182,13 +184,22 @@
     def device(seq, chan):
         return {"seq": seq, "chan": chan}
 
+    fetches = [
+        pltpu.make_async_copy(far, near, fetched.at[n])
+        for n, (far, near) in enumerate(
+            ((taps_far, taps), (ig_far, ig), (va_far, va), (ct_far, ct), (og_far, og))
+        )
+    ]
+    for fetch in fetches:
+        fetch.start()
+
     barrier = pltpu.get_barrier_semaphore()
 
     def greet(seq, chan):
         pl.semaphore_signal(barrier, inc=1, device_id=device(seq, chan), device_id_type=MESH)
 
-    def greet_seq(i, _):
-        greet(lax.rem(s + i, SEQ), c)
+    def greet_seq(ahead, i, _):
+        greet(lax.rem(s // 8 + i // 2, 4) * 8 + lax.rem(s // 2 + ahead, 4) * 2 + lax.rem(s + i, 2), c)
         return 0
 
     def greet_chan(i, _):
@@ -203,23 +214,20 @@
 
         return 0
 
-    lax.fori_loop(1, SEQ, greet_seq, 0)
+    for ahead in (2, 1, 3, 0):
+        lax.fori_loop(0 if ahead else 1, 8, functools.partial(greet_seq, ahead), 0)
     lax.fori_loop(1, CHAN, greet_chan, 0)
     greet(2 * f + 1 - half, c)
     lax.fori_loop(0, TAPS, greet_source, 0)
 
-    taps_flat = stack_tokens(taps[...], range(4))
-    row, col = iota((64, 64), 0), iota((64, 64), 1)
-    taps_rows = nt(one_hot(col == (row & 3) * TAPS + (row >> 2)), taps_flat).astype(BF16)
-    for i in range(TAPS):
-        send_h[i] = taps_rows[4 * i : 4 * (i + 1)]
     route[...] = routing()
+    fetches[0].wait()
+    for n in range(4):
+        send_h[:, n, :] = taps[:, LANES * n : LANES * (n + 1)]
+    fetches[1].wait()
+    fetches[2].wait()
     inner = stack_tokens(product(ig, va).astype(BF16), range(4))
     send_x[...] = nt(route[...], inner).astype(BF16).reshape(SEQ, 16, LANES)
-    upstream = stack_tokens(product(ct, og).astype(BF16), (1, 0, 3, 2))
-    upstream = nn(flip(LANES), upstream).astype(BF16)
-    send_u[...] = nt(route[...], upstream).astype(BF16).reshape(SEQ, 16, LANES)
-
     @pl.when(is_self)
     def _():
         pl.semaphore_wait(barrier, 2 * (SEQ - 1) + TAPS - 1)
@@ -234,91 +242,133 @@
             device_id=device(seq, chan), device_id_type=MESH,
         )
 
+    y_at, z_at, core_at = s // 8, (s // 2) % 4, s % 2
+
+    def exchange_part(src, dst, n, slot, steps):
+        def body(i, _):
+            for step in steps:
+                ahead = lax.rem(z_at + step, 4) * 2 + lax.rem(core_at + i, 2)
+                to = lax.rem(y_at + i // 2, 4) * 8 + ahead
+                copy(src.at[slot(to)], dst.at[s], n, to, c).start()
+            return 0
+
+        lax.fori_loop(1 if steps == (0,) else 0, 8, body, 0)
+
     def exchange(src, dst, n, slot):
-        def body(i, _):
-            to = lax.rem(s + i, SEQ)
-            copy(src.at[slot(to)], dst.at[s], n, to, c).start()
-            return 0
-
-        lax.fori_loop(1, SEQ, body, 0)
+        for steps in ((2,), (1, 3), (0,)):
+            exchange_part(src, dst, n, slot, steps)
         dst[s] = src[slot(s)]
 
     def whole(ref, count, n):
         part = ref.at[pl.ds(0, count)]
         return copy(part, part, n, s, c)
 
-    exchange(send_h, recv_h, 0, lambda to: to // 2)
-    exchange(send_x, recv_x, 1, lambda to: to)
-    exchange(send_u, recv_u, 2, lambda to: to)
-
-    whole(recv_h, SEQ - 1, 0).wait_recv()
-    toeplitz(recv_h, w)
-    whole(recv_x, SEQ - 1, 1).wait_recv()
-    spread_x(unpack(recv_x), xs)
-    convolve(xs, w, y)
-    send_c[...] = pack(y[...])
-    exchange(send_c, recv_c, 3, lambda to: to)
-
-    whole(recv_u, SEQ - 1, 2).wait_recv()
-    u = unpack(recv_u)
-    spread_u(u, us)
-    ut[...] = nt(eye(ROWS), u.astype(BF16)).astype(BF16)
-    convolve_back(us, w, y)
-    send_b[...] = pack(y[...])
-    exchange(send_b, recv_b, 4, lambda to: to)
-
-    correlate(ut, xs, send_g)
-
-    def parts_out(i, _):
-        to = lax.rem(c + i, CHAN)
-        here = c * 2 + half
-
-        @pl.when(i > 0)
+    def send_taps():
+        exchange(send_h, recv_h, 0, lambda to: to // 2)
+
+    def send_inner():
+        exchange(send_x, recv_x, 1, lambda to: to)
+
+    def send_upstream():
+        fetches[3].wait()
+        fetches[4].wait()
+        upstream = stack_tokens(product(ct, og).astype(BF16), (1, 0, 3, 2))
+        upstream = nn(flip(LANES), upstream).astype(BF16)
+        send_u[...] = nt(route[...], upstream).astype(BF16).reshape(SEQ, 16, LANES)
+        exchange(send_u, recv_u, 2, lambda to: to)
+
+    def take_taps():
+        whole(recv_h, SEQ - 1, 0).wait_recv()
+        toeplitz(recv_h, w)
+
+    def take_inner():
+        whole(recv_x, SEQ - 1, 1).wait_recv()
+        spread_x(unpack(recv_x), xs)
+
+    def take_upstream():
+        whole(recv_u, SEQ - 1, 2).wait_recv()
+        u = unpack(recv_u)
+        spread_u(u, us)
+        ut[...] = nt(eye(ROWS), u.astype(BF16)).astype(BF16)
+
+    def forward():
+        convolve(xs, w, y)
+        send_c[...] = pack(y[...])
+        exchange(send_c, recv_c, 3, lambda to: to)
+
+    def backward():
+        convolve_back(us, w, y)
+        send_b[...] = pack(y[...])
+
+    def send_backward_far():
+        exchange_part(send_b, recv_b, 4, lambda to: to, (2,))
+
+    def send_backward_near():
+        exchange_part(send_b, recv_b, 4, lambda to: to, (1, 3))
+        exchange_part(send_b, recv_b, 4, lambda to: to, (0,))
+        recv_b[s] = send_b[s]
+
+    def correlation():
+        correlate(ut, xs, send_g)
+
+        def parts_out(i, _):
+            to = lax.rem(c + i, CHAN)
+            here = c * 2 + half
+
+            @pl.when(i > 0)
+            def _():
+                copy(send_g.at[2 + 16 * half + to], recv_g.at[here], 5, s, to).start()
+
+            other = 1 - half
+            copy(send_g.at[2 + 16 * other + to], recv_g.at[here], 5, 2 * f + other, to).start()
+            return 0
+
+        lax.fori_loop(0, CHAN, parts_out, 0)
+        recv_g[c * 2 + half] = send_g[2 + own_part]
+
+    def totals():
+        whole(recv_g, SEQ - 1, 5).wait_recv()
+        send_t[0] = jnp.sum(recv_g[...], axis=0)
+
+        def total_out(i, _):
+            to = lax.rem(c + i, CHAN)
+
+            @pl.when(jnp.logical_not(jnp.logical_and(is_self, i == 0)))
+            def _():
+                copy(send_t.at[0], recv_t.at[f], 6, own_part, to).start()
+
+            return 0
+
+        lax.fori_loop(0, CHAN, total_out, 0)
+
+        @pl.when(is_self)
         def _():
-            copy(send_g.at[2 + 16 * half + to], recv_g.at[here], 5, s, to).start()
-
-        other = 1 - half
-        copy(send_g.at[2 + 16 * other + to], recv_g.at[here], 5, 2 * f + other, to).start()
-        return 0
-
-    lax.fori_loop(0, CHAN, parts_out, 0)
-    recv_g[c * 2 + half] = send_g[2 + own_part]
+            recv_t[f] = send_t[0]
+
+    send_taps()
+    send_inner()
+    send_upstream()
+    take_taps()
+    take_inner()
+    forward()
+    take_upstream()
+    correlation()
+    backward()
+    send_backward_far()
+    totals()
+    send_backward_near()
 
     whole(recv_c, SEQ - 1, 3).wait_recv()
     tokens = nt(eye(LANES), recv_c[...].reshape(512, LANES)).astype(BF16)
     result = nn(tokens, route[...])
     for n in range(4):
-        here = pl.ds(LANES * (n ^ 1), LANES)
-        part = result[:, LANES * n : LANES * (n + 1)]
-        layer_out[here, :] = (og[here, :].astype(F32) * part).astype(BF16)
-        outer_grad[here, :] = (ct[here, :].astype(F32) * part).astype(BF16)
-
-    whole(recv_g, SEQ - 1, 5).wait_recv()
-    send_t[0] = jnp.sum(recv_g[...], axis=0)
-
-    def total_out(i, _):
-        to = lax.rem(c + i, CHAN)
-
-        @pl.when(jnp.logical_not(jnp.logical_and(is_self, i == 0)))
-        def _():
-            copy(send_t.at[0], recv_t.at[f], 6, own_part, to).start()
-
-        return 0
-
-    lax.fori_loop(0, CHAN, total_out, 0)
-
-    @pl.when(is_self)
-    def _():
-        recv_t[f] = send_t[0]
+        sums[pl.ds(LANES * (n ^ 1), LANES), :] = result[:, LANES * n : LANES * (n + 1)].astype(BF16)
 
     whole(recv_b, SEQ - 1, 4).wait_recv()
     tokens = nt(flip(LANES), recv_b[...].reshape(512, LANES)).astype(BF16)
     result = nn(tokens, route[...])
     for n in range(4):
-        here = pl.ds(LANES * n, LANES)
-        part = result[:, LANES * n : LANES * (n + 1)]
-        inner_grad[here, :] = (part * va[here, :].astype(F32)).astype(BF16)
-        value_grad[here, :] = (part * ig[here, :].astype(F32)).astype(BF16)
+        sums[pl.ds(512 + LANES * n, LANES), :] = result[:, LANES * n : LANES * (n + 1)].astype(BF16)
 
     @pl.when(is_self)
     def _():
@@ -328,29 +378,41 @@
     def _():
         whole(recv_t, TAPS, 6).wait()
 
+    grads[...] = recv_t[...]
+    whole(recv_h, SEQ - 1, 0).wait_send()
+    for n, ref in ((1, recv_x), (2, recv_u), (3, recv_c), (4, recv_b), (5, recv_g)):
+        whole(ref, SEQ - 1, n).wait_send()
+
+
+def finish(sums, grads, og, ig, va, ct, layer_out, outer_grad, inner_grad, value_grad, filter_grad):
+    convolved, backward = sums[0:512].astype(F32), sums[512:].astype(F32)
+    layer_out[...] = (og[...].astype(F32) * convolved).astype(BF16)
+    outer_grad[...] = (ct[...].astype(F32) * convolved).astype(BF16)
+    inner_grad[...] = (backward * va[...].astype(F32)).astype(BF16)
+    value_grad[...] = (backward * ig[...].astype(F32)).astype(BF16)
     scale = float(512 * SEQ * LANES * CHAN // TAPS) ** -0.5
     back = flip(LANES).astype(F32)
     for n in range(4):
         part = lax.dot_general(
-            back, recv_t[:, n, :], (((1,), (1,)), ((), ())),
+            grads[:, n, :], back, (((1,), (0,)), ((), ())),
             precision=lax.Precision.HIGHEST, preferred_element_type=F32,
         )
-        filter_grad[LANES * n : LANES * (n + 1), :] = part * scale
-
-    whole(recv_h, SEQ - 1, 0).wait_send()
-    for n, ref in ((1, recv_x), (2, recv_u), (3, recv_c), (4, recv_b), (5, recv_g)):
-        whole(ref, SEQ - 1, n).wait_send()
+        filter_grad[:, LANES * n : LANES * (n + 1)] = part * scale
 
 
 def on_device(outer_gate, inner_gate, values, filters, cotangent):
     wide = jax.ShapeDtypeStruct((512, LANES), BF16)
     slots = pltpu.VMEM((SEQ, 16, LANES), BF16)
+    near = pltpu.VMEM((512, LANES), BF16)
     vmem = pl.BlockSpec(memory_space=pltpu.VMEM)
-    return pl.pallas_call(
+    sums, grads = pl.pallas_call(
         kernel,
-        out_shape=(wide, wide, wide, wide, jax.ShapeDtypeStruct((512, TAPS), F32)),
-        in_specs=[vmem] * 5,
-        out_specs=(vmem,) * 5,
+        out_shape=(
+            jax.ShapeDtypeStruct((1024, LANES), BF16),
+            jax.ShapeDtypeStruct((TAPS, 4, LANES), F32),
+        ),
+        in_specs=[pl.BlockSpec(memory_space=pltpu.HBM)] * 5,
+        out_specs=(vmem,) * 2,
         scratch_shapes=[
             pltpu.VMEM((TAPS, 4, LANES), BF16),
             slots, slots, slots, slots,
@@ -360,6 +422,9 @@
             slots, slots, slots, slots,
             pltpu.VMEM((SEQ, 4, LANES), F32),
             pltpu.VMEM((TAPS, 4, LANES), F32),
+            near, near, near,
+            pltpu.VMEM((TAPS, 512), BF16),
+            near,
             pltpu.VMEM((129 * LANES, LANES), BF16),
             pltpu.VMEM((2 * ROWS, 1024), BF16),
             pltpu.VMEM((ROWS + 64, 1024), BF16),
@@ -368,11 +433,19 @@
             pltpu.VMEM((512, 512), BF16),
             pltpu.SemaphoreType.DMA((7,)),
             pltpu.SemaphoreType.DMA((7,)),
+            pltpu.SemaphoreType.DMA((5,)),
         ],
         compiler_params=pltpu.CompilerParams(
-            collective_id=0, has_side_effects=True, vmem_limit_bytes=40 * 2**20
+            collective_id=0, has_side_effects=True, vmem_limit_bytes=62 * 2**20
         ),
-    )(outer_gate, inner_gate, values, filters, cotangent)
+    )(outer_gate, inner_gate, values, filters.T, cotangent)
+    *wides, filter_grad = pl.pallas_call(
+        finish,
+        out_shape=(wide, wide, wide, wide, jax.ShapeDtypeStruct((TAPS, 512), F32)),
+        in_specs=[vmem] * 6,
+        out_specs=(vmem,) * 5,
+    )(sums, grads, outer_gate, inner_gate, values, cotangent)
+    return (*wides, filter_grad.T)
 
 
 def solution(mesh):

time: 73.4 us -> 63.1 us (0.86)
  local copies, waits for them, and re-layouts: 6.96 us -> 0 us
  Pallas kernels: 65.6 us -> 62.3 us
    unnamed x13 -> x0, local copies, waits for them, and re-layouts: 6.24 us -> none
    pallas_call x1 -> x2, Pallas kernels: 65.6 us -> 62.3 us  [the longest x1 60 us: on_device(): pl.pallas_call(kernel, out_shape=(jax.ShapeDtypeStruct((1024, LANES), BF1...]
where the time goes in v2:
time: 63.1 us; the launch traced here: 62.9 us
  Pallas kernels  62.3 us (99%)
  between operations  0.64 us (1%)
    pallas_call x1, Pallas kernels, on_device(): pl.pallas_call(kernel, out_shape=(jax.ShapeDtypeStruct((1024, LANES), BF1...  60 us
    pallas_call x1, Pallas kernels, on_device(): pl.pallas_call(finish, out_shape=(wide, wide, wide, wide, jax.ShapeDtypeS...  2.24 us

profile of v2, /device:TPU:1, one launch (start us, length us, event | category | flops | bytes accessed | tf_op | source)
XLA Modules:
  0.0 62.9 jit_solution(16808512149636974144)
XLA Ops:
  0.6 60.0 %shard_map.92 = (bf16[1024,128]{1,0:T(8,128)(2,1)}, f32[16,4,128]{2,1,0:T(4,128)}) custom-call(bf16[512,128]{1,0:T(8,128)(2,1)} %og.1, bf16[512,128]{1,0:T(8,128)(2,1)} %ig.1, bf16[512,128]{1,0:T(8,128)(2,1)} %va.1, bf16[16,512]{1,0:T(8,128)(2,1)} %bitcast.2, bf16[512,128]{1,0:T(8,128)(2,1)} %ct.1), custom_call_target="tpu_custom_call" | custom-call | tf_op jit(solution)/shard_map/pallas_call | solution.py:408
  60.7 2.2 %shard_map.93 = (bf16[512,128]{1,0:T(8,128)(2,1)}, bf16[512,128]{1,0:T(8,128)(2,1)}, bf16[512,128]{1,0:T(8,128)(2,1)}, bf16[512,128]{1,0:T(8,128)(2,1)}, f32[16,512]{1,0:T(8,128)}) custom-call(bf16[1024,128]{1,0:T(8,128)(2,1)} %get-tuple-element.12.sums, f32[16,4,128]{2,1,0:T(4,128)} %get-tuple-element.13.grads, bf16[512,128]{1,0:T(8,128)(2,1)} %og.1, ...), custom_call_target="tpu_custom_call" | custom-call | tf_op jit(solution)/shard_map/pallas_call | solution.py:442

commit v3 on v2

--- a/solution.py
+++ b/solution.py
@@ -215,10 +215,10 @@
         return 0
 
     for ahead in (2, 1, 3, 0):
-        lax.fori_loop(0 if ahead else 1, 8, functools.partial(greet_seq, ahead), 0)
-    lax.fori_loop(1, CHAN, greet_chan, 0)
+        lax.fori_loop(0 if ahead else 1, 8, functools.partial(greet_seq, ahead), 0, unroll=True)
+    lax.fori_loop(1, CHAN, greet_chan, 0, unroll=True)
     greet(2 * f + 1 - half, c)
-    lax.fori_loop(0, TAPS, greet_source, 0)
+    lax.fori_loop(0, TAPS, greet_source, 0, unroll=True)
 
     route[...] = routing()
     fetches[0].wait()
@@ -252,7 +252,7 @@
                 copy(src.at[slot(to)], dst.at[s], n, to, c).start()
             return 0
 
-        lax.fori_loop(1 if steps == (0,) else 0, 8, body, 0)
+        lax.fori_loop(1 if steps == (0,) else 0, 8, body, 0, unroll=True)
 
     def exchange(src, dst, n, slot):
         for steps in ((2,), (1, 3), (0,)):
@@ -323,7 +323,7 @@
             copy(send_g.at[2 + 16 * other + to], recv_g.at[here], 5, 2 * f + other, to).start()
             return 0
 
-        lax.fori_loop(0, CHAN, parts_out, 0)
+        lax.fori_loop(0, CHAN, parts_out, 0, unroll=True)
         recv_g[c * 2 + half] = send_g[2 + own_part]
 
     def totals():
@@ -339,7 +339,7 @@
 
             return 0
 
-        lax.fori_loop(0, CHAN, total_out, 0)
+        lax.fori_loop(0, CHAN, total_out, 0, unroll=True)
 
         @pl.when(is_self)
         def _():

time: 63.1 us -> 61.3 us (0.971)
  Pallas kernels: 62.3 us -> 60.5 us
    pallas_call x1, Pallas kernels: 60 us -> 58.3 us  [on_device(): pl.pallas_call(kernel, out_shape=(jax.ShapeDtypeStruct((1024, LANES), BF1...]
where the time goes in v3:
time: 61.3 us; the launch traced here: 61.2 us
  Pallas kernels  60.5 us (99%)
  between operations  0.64 us (1%)
    pallas_call x1, Pallas kernels, on_device(): pl.pallas_call(kernel, out_shape=(jax.ShapeDtypeStruct((1024, LANES), BF1...  58.3 us
    pallas_call x1, Pallas kernels, on_device(): pl.pallas_call(finish, out_shape=(wide, wide, wide, wide, jax.ShapeDtypeS...  2.24 us

profile of v3, /device:TPU:1, one launch (start us, length us, event | category | flops | bytes accessed | tf_op | source)
XLA Modules:
  0.0 61.2 jit_solution(11366105435912739887)
XLA Ops:
  0.6 58.3 %shard_map.92 = (bf16[1024,128]{1,0:T(8,128)(2,1)}, f32[16,4,128]{2,1,0:T(4,128)}) custom-call(bf16[512,128]{1,0:T(8,128)(2,1)} %og.1, bf16[512,128]{1,0:T(8,128)(2,1)} %ig.1, bf16[512,128]{1,0:T(8,128)(2,1)} %va.1, bf16[16,512]{1,0:T(8,128)(2,1)} %bitcast.2, bf16[512,128]{1,0:T(8,128)(2,1)} %ct.1), custom_call_target="tpu_custom_call" | custom-call | tf_op jit(solution)/shard_map/pallas_call | solution.py:408
  58.9 2.2 %shard_map.93 = (bf16[512,128]{1,0:T(8,128)(2,1)}, bf16[512,128]{1,0:T(8,128)(2,1)}, bf16[512,128]{1,0:T(8,128)(2,1)}, bf16[512,128]{1,0:T(8,128)(2,1)}, f32[16,512]{1,0:T(8,128)}) custom-call(bf16[1024,128]{1,0:T(8,128)(2,1)} %get-tuple-element.12.sums, f32[16,4,128]{2,1,0:T(4,128)} %get-tuple-element.13.grads, bf16[512,128]{1,0:T(8,128)(2,1)} %og.1, ...), custom_call_target="tpu_custom_call" | custom-call | tf_op jit(solution)/shard_map/pallas_call | solution.py:442

commit v4 on v3

--- a/solution.py
+++ b/solution.py
@@ -66,7 +66,7 @@
 
     def body(s, before):
         for n in range(4):
-            h = taps[s, n : n + 1, :].astype(F32)
+            h = taps[s % 2, s // 2, n : n + 1, :].astype(F32)
             now = shear(jnp.broadcast_to(h, (LANES, LANES)))
             at = pl.multiple_of((4 * s + n + 1) * LANES, LANES)
             w[pl.ds(at, LANES), :] = jnp.where(keep, now, before).astype(BF16)
@@ -264,7 +264,16 @@
         return copy(part, part, n, s, c)
 
     def send_taps():
-        exchange(send_h, recv_h, 0, lambda to: to // 2)
+        for ahead in (2, 1, 3, 0):
+            for y_step in range(4):
+                if ahead or y_step:
+                    chip = lax.rem(y_at + y_step, 4) * 4 + lax.rem(z_at + ahead, 4)
+                    copy(send_h.at[chip], recv_h.at[half, f], 0, 2 * chip + half, c).start()
+        recv_h[half, f] = send_h[f]
+
+    def swap_taps():
+        whole(recv_h.at[half], TAPS - 1, 0).wait_recv()
+        return copy(recv_h.at[half], recv_h.at[half], 7, 2 * f + 1 - half, c)
 
     def send_inner():
         exchange(send_x, recv_x, 1, lambda to: to)
@@ -278,7 +287,9 @@
         exchange(send_u, recv_u, 2, lambda to: to)
 
     def take_taps():
-        whole(recv_h, SEQ - 1, 0).wait_recv()
+        swap = swap_taps()
+        swap.start()
+        swap.wait()
         toeplitz(recv_h, w)
 
     def take_inner():
@@ -379,7 +390,7 @@
         whole(recv_t, TAPS, 6).wait()
 
     grads[...] = recv_t[...]
-    whole(recv_h, SEQ - 1, 0).wait_send()
+    whole(recv_h.at[half], TAPS - 1, 0).wait_send()
     for n, ref in ((1, recv_x), (2, recv_u), (3, recv_c), (4, recv_b), (5, recv_g)):
         whole(ref, SEQ - 1, n).wait_send()
 
@@ -418,7 +429,7 @@
             slots, slots, slots, slots,
             pltpu.VMEM((2 + SEQ, 4, LANES), F32),
             pltpu.VMEM((1, 4, LANES), F32),
-            pltpu.VMEM((SEQ, 4, LANES), BF16),
+            pltpu.VMEM((2, TAPS, 4, LANES), BF16),
             slots, slots, slots, slots,
             pltpu.VMEM((SEQ, 4, LANES), F32),
             pltpu.VMEM((TAPS, 4, LANES), F32),
@@ -431,8 +442,8 @@
             pltpu.VMEM((ROWS, ROWS), BF16),
             pltpu.VMEM((ROWS, ROWS), F32),
             pltpu.VMEM((512, 512), BF16),
-            pltpu.SemaphoreType.DMA((7,)),
-            pltpu.SemaphoreType.DMA((7,)),
+            pltpu.SemaphoreType.DMA((8,)),
+            pltpu.SemaphoreType.DMA((8,)),
             pltpu.SemaphoreType.DMA((5,)),
         ],
         compiler_params=pltpu.CompilerParams(

time: 61.3 us -> 60.3 us (0.984)
  Pallas kernels: 60.5 us -> 59.6 us
    pallas_call x1, Pallas kernels: 58.3 us -> 57.3 us  [on_device(): pl.pallas_call(kernel, out_shape=(jax.ShapeDtypeStruct((1024, LANES), BF1...]
where the time goes in v4:
time: 60.3 us; the launch traced here: 60.2 us
  Pallas kernels  59.6 us (99%)
  between operations  0.64 us (1%)
    pallas_call x1, Pallas kernels, on_device(): pl.pallas_call(kernel, out_shape=(jax.ShapeDtypeStruct((1024, LANES), BF1...  57.3 us
    pallas_call x1, Pallas kernels, on_device(): pl.pallas_call(finish, out_shape=(wide, wide, wide, wide, jax.ShapeDtypeS...  2.24 us

profile of v4, /device:TPU:1, one launch (start us, length us, event | category | flops | bytes accessed | tf_op | source)
XLA Modules:
  0.0 60.2 jit_solution(17894041743638079269)
XLA Ops:
  0.6 57.3 %shard_map.92 = (bf16[1024,128]{1,0:T(8,128)(2,1)}, f32[16,4,128]{2,1,0:T(4,128)}) custom-call(bf16[512,128]{1,0:T(8,128)(2,1)} %og.1, bf16[512,128]{1,0:T(8,128)(2,1)} %ig.1, bf16[512,128]{1,0:T(8,128)(2,1)} %va.1, bf16[16,512]{1,0:T(8,128)(2,1)} %bitcast.2, bf16[512,128]{1,0:T(8,128)(2,1)} %ct.1), custom_call_target="tpu_custom_call" | custom-call | tf_op jit(solution)/shard_map/pallas_call | solution.py:419
  58.0 2.2 %shard_map.93 = (bf16[512,128]{1,0:T(8,128)(2,1)}, bf16[512,128]{1,0:T(8,128)(2,1)}, bf16[512,128]{1,0:T(8,128)(2,1)}, bf16[512,128]{1,0:T(8,128)(2,1)}, f32[16,512]{1,0:T(8,128)}) custom-call(bf16[1024,128]{1,0:T(8,128)(2,1)} %get-tuple-element.12.sums, f32[16,4,128]{2,1,0:T(4,128)} %get-tuple-element.13.grads, bf16[512,128]{1,0:T(8,128)(2,1)} %og.1, ...), custom_call_target="tpu_custom_call" | custom-call | tf_op jit(solution)/shard_map/pallas_call | solution.py:453

commit v5 on v4

--- a/solution.py
+++ b/solution.py
@@ -284,11 +284,15 @@
         upstream = stack_tokens(product(ct, og).astype(BF16), (1, 0, 3, 2))
         upstream = nn(flip(LANES), upstream).astype(BF16)
         send_u[...] = nt(route[...], upstream).astype(BF16).reshape(SEQ, 16, LANES)
-        exchange(send_u, recv_u, 2, lambda to: to)
-
-    def take_taps():
+        exchange_part(send_u, recv_u, 2, lambda to: to, (2,))
         swap = swap_taps()
         swap.start()
+        exchange_part(send_u, recv_u, 2, lambda to: to, (1, 3))
+        exchange_part(send_u, recv_u, 2, lambda to: to, (0,))
+        recv_u[s] = send_u[s]
+        return swap
+
+    def take_taps(swap):
         swap.wait()
         toeplitz(recv_h, w)
 
@@ -298,9 +302,7 @@
 
     def take_upstream():
         whole(recv_u, SEQ - 1, 2).wait_recv()
-        u = unpack(recv_u)
-        spread_u(u, us)
-        ut[...] = nt(eye(ROWS), u.astype(BF16)).astype(BF16)
+        ut[...] = nt(eye(ROWS), unpack(recv_u).astype(BF16)).astype(BF16)
 
     def forward():
         convolve(xs, w, y)
@@ -308,6 +310,7 @@
         exchange(send_c, recv_c, 3, lambda to: to)
 
     def backward():
+        spread_u(unpack(recv_u), us)
         convolve_back(us, w, y)
         send_b[...] = pack(y[...])
 
@@ -339,7 +342,7 @@
 
     def totals():
         whole(recv_g, SEQ - 1, 5).wait_recv()
-        send_t[0] = jnp.sum(recv_g[...], axis=0)
+        send_t[0] = jnp.sum(recv_g[...], axis=0).astype(BF16)
 
         def total_out(i, _):
             to = lax.rem(c + i, CHAN)
@@ -358,8 +361,8 @@
 
     send_taps()
     send_inner()
-    send_upstream()
-    take_taps()
+    swap = send_upstream()
+    take_taps(swap)
     take_inner()
     forward()
     take_upstream()
@@ -402,12 +405,8 @@
     inner_grad[...] = (backward * va[...].astype(F32)).astype(BF16)
     value_grad[...] = (backward * ig[...].astype(F32)).astype(BF16)
     scale = float(512 * SEQ * LANES * CHAN // TAPS) ** -0.5
-    back = flip(LANES).astype(F32)
     for n in range(4):
-        part = lax.dot_general(
-            grads[:, n, :], back, (((1,), (0,)), ((), ())),
-            precision=lax.Precision.HIGHEST, preferred_element_type=F32,
-        )
+        part = nn(grads[:, n, :], flip(LANES))
         filter_grad[:, LANES * n : LANES * (n + 1)] = part * scale
 
 
@@ -420,7 +419,7 @@
         kernel,
         out_shape=(
             jax.ShapeDtypeStruct((1024, LANES), BF16),
-            jax.ShapeDtypeStruct((TAPS, 4, LANES), F32),
+            jax.ShapeDtypeStruct((TAPS, 4, LANES), BF16),
         ),
         in_specs=[pl.BlockSpec(memory_space=pltpu.HBM)] * 5,
         out_specs=(vmem,) * 2,
@@ -428,11 +427,11 @@
             pltpu.VMEM((TAPS, 4, LANES), BF16),
             slots, slots, slots, slots,
             pltpu.VMEM((2 + SEQ, 4, LANES), F32),
-            pltpu.VMEM((1, 4, LANES), F32),
+            pltpu.VMEM((1, 4, LANES), BF16),
             pltpu.VMEM((2, TAPS, 4, LANES), BF16),
             slots, slots, slots, slots,
             pltpu.VMEM((SEQ, 4, LANES), F32),
-            pltpu.VMEM((TAPS, 4, LANES), F32),
+            pltpu.VMEM((TAPS, 4, LANES), BF16),
             near, near, near,
             pltpu.VMEM((TAPS, 512), BF16),
             near,

time: 60.3 us -> 59.1 us (0.980)
  Pallas kernels: 59.6 us -> 58 us
    pallas_call x1, Pallas kernels: 57.3 us -> 55.9 us  [on_device(): pl.pallas_call(kernel, out_shape=(jax.ShapeDtypeStruct((1024, LANES), BF1...]
where the time goes in v5:
time: 59.1 us; the launch traced here: 58.6 us
  Pallas kernels  58 us (98%)
  between operations  0.64 us (1%)
    pallas_call x1, Pallas kernels, on_device(): pl.pallas_call(kernel, out_shape=(jax.ShapeDtypeStruct((1024, LANES), BF1...  55.9 us
    pallas_call x1, Pallas kernels, on_device(): pl.pallas_call(finish, out_shape=(wide, wide, wide, wide, jax.ShapeDtypeS...  2.09 us

profile of v5, /device:TPU:1, one launch (start us, length us, event | category | flops | bytes accessed | tf_op | source)
XLA Modules:
  0.0 58.6 jit_solution(3992587362600598156)
XLA Ops:
  0.6 55.9 %shard_map.92 = (bf16[1024,128]{1,0:T(8,128)(2,1)}, bf16[16,4,128]{2,1,0:T(4,128)(2,1)}) custom-call(bf16[512,128]{1,0:T(8,128)(2,1)} %og.1, bf16[512,128]{1,0:T(8,128)(2,1)} %ig.1, bf16[512,128]{1,0:T(8,128)(2,1)} %va.1, bf16[16,512]{1,0:T(8,128)(2,1)} %bitcast.2, bf16[512,128]{1,0:T(8,128)(2,1)} %ct.1), custom_call_target="tpu_custom_call" | custom-call | tf_op jit(solution)/shard_map/pallas_call | solution.py:418
  56.6 2.1 %shard_map.93 = (bf16[512,128]{1,0:T(8,128)(2,1)}, bf16[512,128]{1,0:T(8,128)(2,1)}, bf16[512,128]{1,0:T(8,128)(2,1)}, bf16[512,128]{1,0:T(8,128)(2,1)}, f32[16,512]{1,0:T(8,128)}) custom-call(bf16[1024,128]{1,0:T(8,128)(2,1)} %get-tuple-element.12.sums, bf16[16,4,128]{2,1,0:T(4,128)(2,1)} %get-tuple-element.13.grads, bf16[512,128]{1,0:T(8,128)(2,1)} %og.1, ...), custom_call_target="tpu_custom_call" | custom-call | tf_op jit(solution)/shard_map/pallas_call | solution.py:452

commit v6 on v5

--- a/solution.py
+++ b/solution.py
@@ -73,7 +73,7 @@
             before = now
         return before
 
-    lax.fori_loop(0, SEQ, body, jnp.zeros((LANES, LANES), F32), unroll=8)
+    lax.fori_loop(0, SEQ, body, jnp.zeros((LANES, LANES), F32), unroll=16)
 
 
 def unpack(slots):
@@ -228,6 +228,12 @@
     fetches[2].wait()
     inner = stack_tokens(product(ig, va).astype(BF16), range(4))
     send_x[...] = nt(route[...], inner).astype(BF16).reshape(SEQ, 16, LANES)
+    fetches[3].wait()
+    fetches[4].wait()
+    upstream = stack_tokens(product(ct, og).astype(BF16), (1, 0, 3, 2))
+    upstream = nn(flip(LANES), upstream).astype(BF16)
+    send_u[...] = nt(route[...], upstream).astype(BF16).reshape(SEQ, 16, LANES)
+
     @pl.when(is_self)
     def _():
         pl.semaphore_wait(barrier, 2 * (SEQ - 1) + TAPS - 1)
@@ -279,11 +285,6 @@
         exchange(send_x, recv_x, 1, lambda to: to)
 
     def send_upstream():
-        fetches[3].wait()
-        fetches[4].wait()
-        upstream = stack_tokens(product(ct, og).astype(BF16), (1, 0, 3, 2))
-        upstream = nn(flip(LANES), upstream).astype(BF16)
-        send_u[...] = nt(route[...], upstream).astype(BF16).reshape(SEQ, 16, LANES)
         exchange_part(send_u, recv_u, 2, lambda to: to, (2,))
         swap = swap_taps()
         swap.start()
@@ -398,16 +399,36 @@
         whole(ref, SEQ - 1, n).wait_send()
 
 
-def finish(sums, grads, og, ig, va, ct, layer_out, outer_grad, inner_grad, value_grad, filter_grad):
-    convolved, backward = sums[0:512].astype(F32), sums[512:].astype(F32)
-    layer_out[...] = (og[...].astype(F32) * convolved).astype(BF16)
-    outer_grad[...] = (ct[...].astype(F32) * convolved).astype(BF16)
-    inner_grad[...] = (backward * va[...].astype(F32)).astype(BF16)
-    value_grad[...] = (backward * ig[...].astype(F32)).astype(BF16)
+def finish(
+    sums_far, grads_far, og_far, ig_far, va_far, ct_far,
+    layer_out, outer_grad, inner_grad, value_grad, filter_grad,
+    sums, grads, og, ig, va, ct, out_0, out_1, out_2, out_3, out_4, fetched, stored,
+):
+    sources = (grads_far, sums_far, og_far, ct_far, va_far, ig_far)
+    fetches = [
+        pltpu.make_async_copy(far, near, fetched.at[n])
+        for n, (far, near) in enumerate(zip(sources, (grads, sums, og, ct, va, ig)))
+    ]
+    results = (layer_out, outer_grad, inner_grad, value_grad, filter_grad)
+    stores = [
+        pltpu.make_async_copy(near, far, stored.at[n])
+        for n, (near, far) in enumerate(zip((out_0, out_1, out_2, out_3, out_4), results))
+    ]
+    for fetch in fetches:
+        fetch.start()
     scale = float(512 * SEQ * LANES * CHAN // TAPS) ** -0.5
+    fetches[0].wait()
     for n in range(4):
-        part = nn(grads[:, n, :], flip(LANES))
-        filter_grad[:, LANES * n : LANES * (n + 1)] = part * scale
+        out_4[:, LANES * n : LANES * (n + 1)] = nn(grads[:, n, :], flip(LANES)) * scale
+    stores[4].start()
+    fetches[1].wait()
+    for n, (gate, out) in enumerate(((og, out_0), (ct, out_1), (va, out_2), (ig, out_3))):
+        fetches[2 + n].wait()
+        half = sums[512 * (n // 2) : 512 * (n // 2 + 1)]
+        out[...] = (gate[...].astype(F32) * half.astype(F32)).astype(BF16)
+        stores[n].start()
+    for store in stores:
+        store.wait()
 
 
 def on_device(outer_gate, inner_gate, values, filters, cotangent):
@@ -452,8 +473,17 @@
     *wides, filter_grad = pl.pallas_call(
         finish,
         out_shape=(wide, wide, wide, wide, jax.ShapeDtypeStruct((TAPS, 512), F32)),
-        in_specs=[vmem] * 6,
-        out_specs=(vmem,) * 5,
+        in_specs=[pl.BlockSpec(memory_space=pl.ANY)] * 6,
+        out_specs=(pl.BlockSpec(memory_space=pl.ANY),) * 5,
+        scratch_shapes=[
+            pltpu.VMEM((1024, LANES), BF16),
+            pltpu.VMEM((TAPS, 4, LANES), BF16),
+            *[near] * 8,
+            pltpu.VMEM((TAPS, 512), F32),
+            pltpu.SemaphoreType.DMA((6,)),
+            pltpu.SemaphoreType.DMA((5,)),
+        ],
+        compiler_params=pltpu.CompilerParams(vmem_limit_bytes=62 * 2**20),
     )(sums, grads, outer_gate, inner_gate, values, cotangent)
     return (*wides, filter_grad.T)
 

time: 59.1 us -> 59 us (level)
  no operation moved by 1% of the time
where the time goes in v6:
time: 59 us; the launch traced here: 58.6 us
  Pallas kernels  58 us (98%)
  between operations  0.64 us (1%)
    pallas_call x1, Pallas kernels, on_device(): pl.pallas_call(kernel, out_shape=(jax.ShapeDtypeStruct((1024, LANES), BF1...  56 us
    pallas_call x1, Pallas kernels, on_device(): pl.pallas_call(finish, out_shape=(wide, wide, wide, wide, jax.ShapeDtypeS...  1.96 us

profile of v6, /device:TPU:1, one launch (start us, length us, event | category | flops | bytes accessed | tf_op | source)
XLA Modules:
  0.0 58.6 jit_solution(10100453875320370363)
XLA Ops:
  0.6 56.0 %shard_map.92 = (bf16[1024,128]{1,0:T(8,128)(2,1)}, bf16[16,4,128]{2,1,0:T(4,128)(2,1)}) custom-call(bf16[512,128]{1,0:T(8,128)(2,1)} %og_far.3, bf16[512,128]{1,0:T(8,128)(2,1)} %ig_far.3, bf16[512,128]{1,0:T(8,128)(2,1)} %va_far.3, bf16[16,512]{1,0:T(8,128)(2,1)} %bitcast.2, bf16[512,128]{1,0:T(8,128)(2,1)} %ct_far.3), custom_call_target="tpu_custom_call" | custom-call | tf_op jit(solution)/shard_map/pallas_call | solution.py:439
  56.6 2.0 %shard_map.93 = (bf16[512,128]{1,0:T(8,128)(2,1)}, bf16[512,128]{1,0:T(8,128)(2,1)}, bf16[512,128]{1,0:T(8,128)(2,1)}, bf16[512,128]{1,0:T(8,128)(2,1)}, f32[16,512]{1,0:T(8,128)}) custom-call(bf16[1024,128]{1,0:T(8,128)(2,1)} %get-tuple-element.12.sums_far, bf16[16,4,128]{2,1,0:T(4,128)(2,1)} %get-tuple-element.13.grads_far, bf16[512,128]{1,0:T(8,128)(2,1)} %og_far.3, ...), custom_call_target="tpu_custom_call" | custom-call | tf_op jit(solution)/shard_map/pallas_call | solution.py:473
